TPU v7x, 32 devices: a whole 2x2x4 slice. The times are simulated.
32 devices in a mesh: grp: 2 (over x), ctx: 16 (over z, y, core).
Axes of the slice: x: 2, y: 2, z: 4, core: 2. Of those that a mesh axis runs over, the one named last changes fastest.
Arguments:
- queries: bfloat16 [2, 4096, 1536], P(None, ('grp', 'ctx')), parts along dimension 1, may hold values from -6 to 6
- keys: bfloat16 [4096, 1536], P(('grp', 'ctx')), parts along dimension 0, may hold values from -6 to 6
- values: bfloat16 [4096, 1536], P(('grp', 'ctx')), parts along dimension 0, may hold values from -6 to 6
- lr_tok: float32 [4096, 4], P(('grp', 'ctx')), parts along dimension 0, as said below
- lr_base: float32 [4], replicated, may hold values from 0.5 to 2
- fast_init: bfloat16 [4608, 384], replicated, may hold values from -0.3125 to 0.3125
- fast_saved: bfloat16 [9216, 384], P(('grp', 'ctx')), parts along dimension 0, may hold values from -0.3125 to 0.3125
- dout: bfloat16 [2, 4096, 1536], P(None, ('grp', 'ctx')), parts along dimension 1, may hold values from -0.59765625 to 0.59765625
Outputs:
- d_queries: bfloat16 [2, 4096, 1536], P(None, ('grp', 'ctx')), parts along dimension 1
- d_keys: bfloat16 [4096, 1536], P(('grp', 'ctx')), parts along dimension 0
- d_values: bfloat16 [4096, 1536], P(('grp', 'ctx')), parts along dimension 0
- d_lr_tok: float32 [4096, 4], P(('grp', 'ctx')), parts along dimension 0
- d_lr_base: float32 [8], P('grp'), parts along dimension 0
- d_fast_init: float32 [9216, 384], P(('grp', 'ctx')), parts along dimension 0
There are 2 independent parts, one for each index of `grp`. A program takes and returns all parts, laid end to end along the dimension named above; an argument that names none is the same for every part. Nothing has to cross between parts.
Inputs may be any that keep to these rules, and one draw needn't show every extreme that they name: `lr_tok`: positive rates.
All inputs are finite; a program needn't handle non-finite values.
Results may differ from a plain program's by a relative error of at most 0.0012.
Values may be sent and summed in bfloat16 or wider, within the bound.
A program may use at most 128 MiB of HBM per device.

v0:
```python
import jax
import jax.numpy as jnp
from jax import lax
from jax.sharding import PartitionSpec as P


def contract(form, left, right):
    return jnp.einsum(form, left, right, precision=lax.Precision.HIGHEST)


def split_heads(tokens_in, head_count):
    return tokens_in.astype(jnp.float32).reshape(tokens_in.shape[0], head_count, -1)


def forward_parts(weights, inputs):
    gate_value = contract("thd,hde->the", inputs, weights[0])
    up_value = contract("thd,hde->the", inputs, weights[1])
    logistic = jax.nn.sigmoid(gate_value)
    activated = gate_value * logistic
    hidden = activated * up_value
    return (gate_value, up_value, logistic, activated, hidden)


def query_adjoint(weights, inputs, cotangent):
    gate_value, up_value, logistic, activated, hidden = forward_parts(weights, inputs)
    d_hidden = contract("thf,hef->the", cotangent, weights[2])
    slope_one = logistic * (1.0 + gate_value * (1.0 - logistic))
    d_gate = d_hidden * up_value * slope_one
    d_up = d_hidden * activated
    first_rows = contract("thd,the->hde", inputs, d_gate)
    third_rows = contract("thd,the->hde", inputs, d_up)
    second_rows = contract("the,thf->hef", hidden, cotangent)
    d_inputs = contract("the,hde->thd", d_gate, weights[0]) + contract(
        "the,hde->thd", d_up, weights[1]
    )
    return (jnp.stack([first_rows, third_rows, second_rows]), d_inputs)


def second_order(weights, adjoint, key_heads, value_heads, token_rates):
    gate_value, up_value, logistic, activated, hidden = forward_parts(weights, key_heads)
    scaled = token_rates[:, :, None] * value_heads
    d_hidden = contract("thf,hef->the", scaled, weights[2])
    slope_one = logistic * (1.0 + gate_value * (1.0 - logistic))
    curvature = logistic * (1.0 - logistic) * (2.0 + gate_value * (1.0 - 2.0 * logistic))
    proj_one = contract("thd,hde->the", key_heads, adjoint[0])
    proj_three = contract("thd,hde->the", key_heads, adjoint[1])
    mixed_term = proj_one * up_value * slope_one + proj_three * activated
    back_two = contract("thf,hef->the", scaled, adjoint[2])
    d_scaled = contract("the,hef->thf", mixed_term, weights[2]) + contract(
        "the,hef->thf", hidden, adjoint[2]
    )
    second_rows = contract("the,thf->hef", mixed_term, scaled)
    bar_gate = (
        d_hidden * (proj_one * up_value * curvature + proj_three * slope_one)
        + back_two * up_value * slope_one
    )
    bar_up = d_hidden * proj_one * slope_one + back_two * activated
    first_rows = contract("thd,the->hde", key_heads, bar_gate)
    third_rows = contract("thd,the->hde", key_heads, bar_up)
    key_grad = contract("the,hde->thd", bar_gate, weights[0]) + contract(
        "the,hde->thd", bar_up, weights[1]
    )
    key_grad = key_grad + contract("the,hde->thd", d_hidden * up_value * slope_one, adjoint[0])
    key_grad = key_grad + contract("the,hde->thd", d_hidden * activated, adjoint[1])
    value_grad = token_rates[:, :, None] * d_scaled
    rate_grad = jnp.sum(value_heads * d_scaled, axis=2)
    return (jnp.stack([first_rows, third_rows, second_rows]), key_grad, value_grad, rate_grad)


def local(queries, keys, values, lr_tok, lr_base, fast_init, fast_saved, dout):
    head_count = lr_base.shape[0]
    head_size = fast_init.shape[1]
    shape_four = (3, head_count, head_size, head_size)
    share_rows = fast_saved.shape[0]
    fast_zero = fast_init.astype(jnp.float32).reshape(shape_four)
    gathered = lax.all_gather(fast_saved, "ctx", axis=0, tiled=True)
    fast_one = gathered.astype(jnp.float32).reshape(shape_four)
    grad_one, query_one = query_adjoint(
        fast_one, split_heads(queries[1], head_count), split_heads(dout[1], head_count)
    )
    flat_one = grad_one.reshape(-1, head_size)
    summed_one = lax.psum(flat_one, "ctx")
    carried = lax.dynamic_slice_in_dim(
        summed_one, lax.axis_index("ctx") * share_rows, share_rows, 0
    )
    direction = summed_one.reshape(shape_four)
    grad_zero, query_zero = query_adjoint(
        fast_zero, split_heads(queries[0], head_count), split_heads(dout[0], head_count)
    )
    key_heads = split_heads(keys, head_count)
    value_heads = split_heads(values, head_count)
    token_rates = lr_tok * lr_base[None, :]
    second, key_grad, value_grad, rate_grad = second_order(
        fast_zero, direction, key_heads, value_heads, token_rates
    )
    base_grad = lax.psum(jnp.sum(rate_grad * lr_tok, axis=0), "ctx")
    local_term = (second + grad_zero).reshape(-1, head_size)
    d_fast = carried + lax.psum_scatter(local_term, "ctx", scatter_dimension=0, tiled=True)
    token_count = queries.shape[1]
    d_queries = jnp.stack([query_zero, query_one]).reshape(2, token_count, -1).astype(jnp.bfloat16)
    d_keys = key_grad.reshape(token_count, -1).astype(jnp.bfloat16)
    d_values = value_grad.reshape(token_count, -1).astype(jnp.bfloat16)
    d_lr_tok = rate_grad * lr_base[None, :]
    return (d_queries, d_keys, d_values, d_lr_tok, base_grad, d_fast)


def solution(mesh):
    in_specs = (
        P(None, ("grp", "ctx"), None),
        P(("grp", "ctx"), None),
        P(("grp", "ctx"), None),
        P(("grp", "ctx"), None),
        P(),
        P(),
        P(("grp", "ctx"), None),
        P(None, ("grp", "ctx"), None),
    )
    out_specs = (
        P(None, ("grp", "ctx"), None),
        P(("grp", "ctx"), None),
        P(("grp", "ctx"), None),
        P(("grp", "ctx"), None),
        P("grp"),
        P(("grp", "ctx"), None),
    )
    return jax.shard_map(local, mesh=mesh, in_specs=in_specs, out_specs=out_specs, check_vma=False)
```

profile of v0, /device:TPU:0, one launch (start us, length us, event | category | flops | bytes accessed | tf_op | source)
XLA Modules:
  0.0 340.8 jit_solution(2358670516625425250)
XLA Ops:
  7.2 0.7 all-gather.2.cloned.1.call-update
  8.0 1.2 fusion.50
  9.6 50.6 %all-gather.2.cloned.1.call-done = bf16[4608,384]{1,0:T(8,128)(2,1)} async-done(((bf16[288,384]{1,0:T(8,128)(2,1)}), bf16[4608,384]{1,0:T(8,128)(2,1)}) %all-gather.2.cloned.1.call-update) | async-done | bytes 3538960 | tf_op jit(solution)/shard_map/all_gather | solution.py:76
  60.2 2.3 fusion.48
  64.4 1.1 convolution_bitcast_fusion.6
  65.6 1.2 convolution_bitcast_fusion.7
  66.8 1.3 convolution_bitcast_fusion.8
  68.1 3.4 pad_maximum_fusion
  71.8 0.9 copy.148
  72.8 0.9 copy.147
  74.4 2.9 fusion.47
  77.9 0.5 convolution_bitcast_fusion.19
  78.6 2.6 convolution_bitcast_fusion
  81.7 2.6 convolution_bitcast_fusion.1
  84.2 1.4 convolution_bitcast_fusion.13
  85.7 1.4 convolution_bitcast_fusion.14
  87.1 2.1 convolution_bitcast_fusion.24
  89.2 2.7 convolution_bitcast_fusion.2
  91.9 129.1 %all-reduce.2.cloned.1.call-done = f32[4608,384]{1,0:T(8,128)} async-done(((f32[4608,384]{1,0:T(8,128)}), f32[4608,384]{1,0:T(8,128)}) %all-reduce.2.cloned.1.call-update) | async-done | bytes 7077904 | tf_op jit(solution)/shard_map/psum | solution.py:82
  221.0 3.5 %fusion.46 = (f32[1536,384]{1,0:T(8,128)S(1)}, f32[1536,384]{1,0:T(8,128)S(1)}, f32[1536,384]{1,0:T(8,128)S(1)}) fusion(f32[4608,384]{1,0:T(8,128)} %all-reduce.2.cloned.1.call-done), kind=kLoop, calls=%fused_computation.83 | loop fusion | bytes 14155776 | tf_op jit(solution)/shard_map/slice | solution.py:48
  224.6 2.1 convolution_bitcast_fusion.22
  226.7 3.0 convolution_bitcast_fusion.12
  229.7 2.6 multiply_add_fusion
  232.3 2.1 convolution_bitcast_fusion.3
  234.5 1.1 convolution_bitcast_fusion.4
  235.6 1.1 convolution_bitcast_fusion.5
  236.8 1.0 copy-done.22
  237.8 3.5 %maximum_add_fusion = f32[3,4,384,384]{3,2,1,0:T(8,128)} fusion(f32[1,4,384,384]{3,2,1,0:T(8,128)S(1)} %convolution_bitcast_fusion.3, f32[1,4,384,384]{3,2,1,0:T(8,128)S(1)} %convolution_bitcast_fusion.4, f32[1,4,384,384]{3,2,1,0:T(8,128)S(1)} %convolution_bitcast_fusion.5, f32[1,4,384,384]{3,2,1,0:T(8,128)S(1)} %copy-done.23, ...), kind=kLoop, calls=%fused_computation.1 | loop fusion | flops 8847360 | bytes 21233664 | tf_op jit(solution)/shard_map/add | solution.py:97
  241.3 3.7 %fusion.41 = f32[4,128,384]{2,1,0:T(8,128)S(1)} fusion(bf16[4,384,384]{2,1,0:T(8,128)(2,1)} %bitcast.164, f32[128,4,384]{0,2,1:T(8,128)} %copy-done.19, f32[128,4,384]{0,2,1:T(8,128)} %copy-done.33, f32[128,4,384]{0,2,1:T(8,128)} %copy-done.32), kind=kOutput, calls=%fused_computation.81 | convolution fusion | flops 907739136 | bytes 4325376 | tf_op jit(solution)/shard_map/the,hde->thd/dot_general | solution.py:8
  245.0 2.3 fusion.8
  247.3 1.2 copy.62
  248.6 4.0 %fusion.42 = f32[4,128,384]{2,1,0:T(8,128)S(1)} fusion(bf16[4,384,384]{2,1,0:T(8,128)(2,1)} %bitcast.180, f32[128,4,384]{0,2,1:T(8,128)} %copy-done.17, f32[128,4,384]{0,2,1:T(8,128)} %copy-done.29, f32[128,4,384]{0,2,1:T(8,128)} %copy-done.31), kind=kOutput, calls=%fused_computation.82 | convolution fusion | flops 907739136 | bytes 4325376 | tf_op jit(solution)/shard_map/the,hde->thd/dot_general | solution.py:8
  252.6 2.3 fusion.7
  254.9 1.9 copy.72
  256.8 2.0 pad_maximum_fusion.1
  258.8 2.3 copy.107
  261.2 2.8 convolution_bitcast_fusion.23
  264.0 2.3 multiply_reduce_fusion
  266.3 0.8 multiply_reduce_fusion.1
  267.1 34.3 %psum.15 = f32[4]{0:T(128)} all-reduce(f32[4]{0:T(128)S(1)} %get-tuple-element.30), channel_id=1, replica_groups=mesh['grp'=2,'ctx'=16] {'ctx'}, use_global_device_ids=true, to_apply=%region_3.0 | all-reduce | flops 4 | bytes 32 | tf_op jit(solution)/shard_map/psum | solution.py:96
  301.4 3.0 fusion.51
  304.4 4.2 %convolution_bitcast_fusion.10 = f32[128,4,384]{2,0,1:T(8,128)S(1)} fusion(f32[4,384,384]{2,1,0:T(8,128)S(1)} %bitcast.151, f32[128,4,384]{0,2,1:T(8,128)} %convolution_bitcast_fusion.24, f32[128,4,384]{0,2,1:T(8,128)} %convolution_bitcast_fusion.13), kind=kOutput, calls=%fused_computation.12 | convolution fusion | flops 906952704 | bytes 4718592 | tf_op jit(solution)/shard_map/the,hde->thd/dot_general | solution.py:8
  308.7 2.7 convolution_bitcast_fusion.11
  311.4 1.5 fusion.4
  313.1 0.9 copy.108
  314.3 0.9 copy.109
  315.2 16.9 %reduce-scatter.2.cloned.1.call-done = f32[288,384]{1,0:T(8,128)} async-done(((f32[4608,384]{1,0:T(8,128)}), f32[288,384]{1,0:T(8,128)}) %reduce-scatter.2.cloned.1.call-update) | async-done | bytes 442384 | tf_op jit(solution)/shard_map/reduce_scatter | solution.py:98
  332.1 2.0 dynamic-slice_add_fusion
  (106 shorter events, 5.3 us)
Async XLA Ops:
  7.2 2.2 copy-start.39
  7.2 53.0 %all-gather.2.cloned.1.call-start = ((), (), s32[]{:S(2)}) async-start(), calls=%async_computation.1 | async-start | bytes 3760128 | tf_op jit(solution)/shard_map/all_gather | solution.py:76
  7.9 213.1 %all-reduce.2.cloned.1.call-start = ((), (), s32[]{:S(2)}) async-start(), calls=%async_computation.2 | async-start | bytes 14155776 | tf_op jit(solution)/shard_map/psum | solution.py:82
  62.6 1.1 copy-start.35
  62.6 1.4 copy-start.37
  63.1 3.6 %copy-start.17 = (f32[128,4,384]{0,2,1:T(8,128)}, f32[128,4,384]{0,2,1:T(8,128)S(1)}, u32[]{:S(2)}) copy-start(f32[128,4,384]{0,2,1:T(8,128)S(1)} %convolution_bitcast_fusion.15) | copy-start | bytes 2359300
  64.0 2.8 copy-start.31
  64.4 2.4 copy-start.29
  71.4 2.2 copy-start.40
  71.5 2.6 copy-start.41
  71.5 2.9 copy-start.42
  71.5 2.9 copy-start.43
  71.5 260.6 %reduce-scatter.2.cloned.1.call-start = ((), (), s32[]{:S(2)}) async-start(), calls=%async_computation.3 | async-start | bytes 7520256 | tf_op jit(solution)/shard_map/reduce_scatter | solution.py:98
  74.4 2.9 copy-start.21
  77.3 6.9 %copy-start.10 = (bf16[1536,384]{1,0:T(8,128)(2,1)}, bf16[1536,384]{1,0:T(8,128)(2,1)S(1)}, u32[]{:S(2)}) copy-start(bf16[1536,384]{1,0:T(8,128)(2,1)S(1)} %get-tuple-element.17) | copy-start | bytes 3538948
  77.3 8.4 %copy-start.7 = (bf16[1536,384]{1,0:T(8,128)(2,1)}, bf16[1536,384]{1,0:T(8,128)(2,1)S(1)}, u32[]{:S(2)}) copy-start(bf16[1536,384]{1,0:T(8,128)(2,1)S(1)} %get-tuple-element.15) | copy-start | bytes 3538948
  77.3 9.8 %copy-start.11 = (bf16[1536,384]{1,0:T(8,128)(2,1)}, bf16[1536,384]{1,0:T(8,128)(2,1)S(1)}, u32[]{:S(2)}) copy-start(bf16[1536,384]{1,0:T(8,128)(2,1)S(1)} %get-tuple-element.16) | copy-start | bytes 3538948
  77.3 1.3 copy-start.38
  77.9 11.3 %copy-start.19 = (f32[128,4,384]{0,2,1:T(8,128)}, f32[128,4,384]{0,2,1:T(8,128)S(1)}, u32[]{:S(2)}) copy-start(f32[128,4,384]{0,2,1:T(8,128)S(1)} %convolution_bitcast_fusion.18) | copy-start | bytes 2359300
  78.5 10.8 %copy-start.32 = (f32[128,4,384]{0,2,1:T(8,128)}, f32[128,4,384]{0,2,1:T(8,128)S(1)}, u32[]{:S(2)}) copy-start(f32[128,4,384]{0,2,1:T(8,128)S(1)} %convolution_bitcast_fusion.19) | copy-start | bytes 2359300
  81.7 7.6 %copy-start.33 = (f32[128,4,384]{0,2,1:T(8,128)}, f32[128,4,384]{0,2,1:T(8,128)S(1)}, u32[]{:S(2)}) copy-start(f32[128,4,384]{0,2,1:T(8,128)S(1)} %convolution_bitcast_fusion.20) | copy-start | bytes 2359300
  224.6 5.1 %copy-start = (f32[1536,384]{1,0:T(8,128)}, f32[1536,384]{1,0:T(8,128)S(1)}, u32[]{:S(2)}) copy-start(f32[1536,384]{1,0:T(8,128)S(1)} %get-tuple-element.14) | copy-start | bytes 7077892
  224.6 5.1 %copy-start.2 = (f32[1536,384]{1,0:T(8,128)}, f32[1536,384]{1,0:T(8,128)S(1)}, u32[]{:S(2)}) copy-start(f32[1536,384]{1,0:T(8,128)S(1)} %get-tuple-element.13) | copy-start | bytes 7077892
  226.7 3.0 copy-start.4
  226.7 3.0 copy-start.12
  226.7 3.0 copy-start.15
  232.3 3.3 copy-start.25
  232.3 3.3 copy-start.28
  232.3 3.3 copy-start.27
  234.4 2.3 copy-start.23
  234.4 2.4 copy-start.24
  235.6 2.2 copy-start.22
  241.3 3.7 %copy-start.8 = (bf16[1536,384]{1,0:T(8,128)(2,1)S(1)}, bf16[1536,384]{1,0:T(8,128)(2,1)}, u32[]{:S(2)}) copy-start(bf16[1536,384]{1,0:T(8,128)(2,1)} %copy-done.7) | copy-start | bytes 3538948
  241.3 3.7 %copy-start.20 = (f32[128,4,384]{0,2,1:T(8,128)S(1)}, f32[128,4,384]{0,2,1:T(8,128)}, u32[]{:S(2)}) copy-start(f32[128,4,384]{0,2,1:T(8,128)} %copy-done.19) | copy-start | bytes 2359300
  241.3 3.7 %copy-start.34 = (f32[128,4,384]{0,2,1:T(8,128)S(1)}, f32[128,4,384]{0,2,1:T(8,128)}, u32[]{:S(2)}) copy-start(f32[128,4,384]{0,2,1:T(8,128)} %copy-done.33) | copy-start | bytes 2359300
  248.5 4.1 %copy-start.18 = (f32[128,4,384]{0,2,1:T(8,128)S(1)}, f32[128,4,384]{0,2,1:T(8,128)}, u32[]{:S(2)}) copy-start(f32[128,4,384]{0,2,1:T(8,128)} %copy-done.17) | copy-start | bytes 2359300
  248.5 4.1 %copy-start.30 = (f32[128,4,384]{0,2,1:T(8,128)S(1)}, f32[128,4,384]{0,2,1:T(8,128)}, u32[]{:S(2)}) copy-start(f32[128,4,384]{0,2,1:T(8,128)} %copy-done.29) | copy-start | bytes 2359300
  248.5 4.1 %copy-start.36 = (bf16[1536,384]{1,0:T(8,128)(2,1)S(1)}, bf16[1536,384]{1,0:T(8,128)(2,1)}, u32[]{:S(2)}) copy-start(bf16[1536,384]{1,0:T(8,128)(2,1)} %copy-done.35) | copy-start | bytes 3538948
  261.2 2.8 copy-start.5
  261.2 2.8 copy-start.13
  266.3 38.1 %copy-start.3 = (f32[1536,384]{1,0:T(8,128)S(1)}, f32[1536,384]{1,0:T(8,128)}, u32[]{:S(2)}) copy-start(f32[1536,384]{1,0:T(8,128)} %copy-done.2) | copy-start | bytes 7077892
  304.4 4.2 %copy-start.1 = (f32[1536,384]{1,0:T(8,128)S(1)}, f32[1536,384]{1,0:T(8,128)}, u32[]{:S(2)}) copy-start(f32[1536,384]{1,0:T(8,128)} %copy-done) | copy-start | bytes 7077892
  304.4 4.2 %copy-start.6 = (f32[128,4,384]{0,2,1:T(8,128)S(1)}, f32[128,4,384]{0,2,1:T(8,128)}, u32[]{:S(2)}) copy-start(f32[128,4,384]{0,2,1:T(8,128)} %convolution_bitcast_fusion.13) | copy-start | bytes 2359300
  304.4 4.2 %copy-start.14 = (f32[128,4,384]{0,2,1:T(8,128)S(1)}, f32[128,4,384]{0,2,1:T(8,128)}, u32[]{:S(2)}) copy-start(f32[128,4,384]{0,2,1:T(8,128)} %convolution_bitcast_fusion.14) | copy-start | bytes 2359300
  304.4 4.2 %copy-start.16 = (f32[128,4,384]{0,2,1:T(8,128)S(1)}, f32[128,4,384]{0,2,1:T(8,128)}, u32[]{:S(2)}) copy-start(f32[128,4,384]{0,2,1:T(8,128)} %convolution_bitcast_fusion.24) | copy-start | bytes 2359300
  308.6 2.7 copy-start.9
  308.6 2.7 copy-start.26
Sparse Core Ops, SparseCore 0:
  10.3 49.8 all-gather.1
  71.6 149.3 all-reduce.1
  241.4 90.6 reduce-scatter.1
where the time goes:
time: 346 us; the launch traced here: 341 us
  waiting for transfers between devices  197 us (57%)
  matrix products  60.1 us (17%)
  blocking collectives  34.3 us (10%)
  local copies, waits for them, and re-layouts  22.3 us (6%)
  between operations  14.8 us (4%)
  other arithmetic  11.6 us (3%)
    psum x1, waiting for transfers between devices, local(): summed_one = lax.psum(flat_one, 'ctx')  129 us
    dot_general x31, matrix products, contract(): return jnp.einsum(form, left, right, precision=lax.Precision.HIGHEST)  60.1 us
    all_gather x1, waiting for transfers between devices, local(): gathered = lax.all_gather(fast_saved, 'ctx', axis=0, tiled=True)  50.6 us
    psum x1, blocking collectives, local(): base_grad = lax.psum(jnp.sum(rate_grad * lr_tok, axis=0), 'ctx')  34.3 us
    reduce_scatter x1, waiting for transfers between devices, local(): lax.psum_scatter(local_term, 'ctx', scatter_dimension=0, tiled=True)  16.9 us
    unnamed x96, local copies, waits for them, and re-layouts  8.31 us
  transfers between devices with their start and end apart: 3, of which 3 were waited for; matrix products, arithmetic and copies ran while one was open for 18% of the time, Pallas kernels for 0%

commit v1 on v0

v1 whole, which is shorter than its diff:
```python
import functools

import jax
import jax.numpy as jnp
from jax import lax
from jax.experimental import pallas as pl
from jax.experimental.pallas import tpu as pltpu
from jax.sharding import PartitionSpec as P

MESH = pl.DeviceIdType.MESH
BF = jnp.bfloat16
F32 = jnp.float32


def split(x):
    hi = x.astype(BF)
    return hi, (x - hi.astype(F32)).astype(BF)


def dg(a, b, ca, cb):
    return lax.dot_general(a, b, (((ca,), (cb,)), ((), ())), preferred_element_type=F32)


def nn(a, b):
    return dg(a, b, 1, 0)


def nt(a, b):
    return dg(a, b, 1, 1)


def tn(a, b):
    return dg(a, b, 0, 0)


def two(op, a, b):
    if isinstance(a, tuple) and isinstance(b, tuple):
        return op(a[0], b[0]) + (op(a[0], b[1]) + op(a[1], b[0]))
    if isinstance(a, tuple):
        return op(a[0], b) + op(a[1], b)
    return op(a, b[0]) + op(a, b[1])


def gate_terms(gate):
    logistic = 1.0 / (1.0 + jnp.exp(-gate))
    return logistic, gate * logistic, logistic * (1.0 + gate * (1.0 - logistic))


def query_terms(x, g, w1, w3, w2):
    gate, up, d_hidden = nn(x, w1), nn(x, w3), nt(g, w2)
    _, activated, slope = gate_terms(gate)
    return split(d_hidden * up * slope), split(d_hidden * activated), split(activated * up)


class Copy:
    def __init__(self, me, dest, src, dst, send, recv):
        self.away = dest != me
        self.remote = pltpu.make_async_remote_copy(
            src_ref=src, dst_ref=dst, send_sem=send, recv_sem=recv,
            device_id={"ctx": dest}, device_id_type=MESH)
        self.near = pltpu.make_async_copy(src, dst, recv)

    def start(self):
        @pl.when(self.away)
        def _():
            self.remote.start()

        @pl.when(jnp.logical_not(self.away))
        def _():
            self.near.start()

    def wait_send(self):
        @pl.when(self.away)
        def _():
            self.remote.wait_send()


def arrived(buf, sem):
    pltpu.make_async_copy(buf, buf, sem).wait()


def body(sz, q_ref, do_ref, k_ref, v_ref, lr_ref, base_ref, init_ref, saved_ref,
         dq_ref, dk_ref, dv_ref, rate_ref, part_ref, fast_ref,
         line, rest, lrs, w1buf, w0buf, adj, tot, sib, fbuf, stage, rows, tile,
         s_line, r_line, s_fwd, r_fwd, s_sib, r_sib, s_rest, r_rest, s_lr, r_lr,
         s_w, r_w, s_wf, r_init, s_out, r_out, s_rate, r_rate, s_tile, r_tile,
         s_half, r_half, s_fin, r_fin):
    n, heads, group, chips, tb, dh, grain, k, pieces = sz
    me = lax.axis_index("ctx")
    h = me // group
    j = lax.rem(me, group)
    chip, core = j // 2, lax.rem(j, 2)
    other = h * group + chip * 2 + (1 - core)
    own = pieces

    def cols(i):
        return pl.ds(pl.multiple_of(i * dh, 128), dh)

    barrier = pltpu.get_barrier_semaphore()
    for step in range(1, n):
        pl.semaphore_signal(barrier, inc=1, device_id={"ctx": lax.rem(me + step, n)},
                            device_id_type=MESH)
    init_copies = [pltpu.make_async_copy(
        init_ref.at[pl.ds(pl.multiple_of((m * heads + h) * dh, 16), dh)], w0buf.at[m], r_init.at[m])
        for m in range(3)]
    for c in init_copies:
        c.start()
    pl.semaphore_wait(barrier, n - 1)

    sends = []

    def go(copy):
        copy.start()
        sends.append(copy)

    for step in (2, 1, 3, 0):
        hh = lax.rem(h + step, heads)
        for t, ref in ((0, q_ref), (1, do_ref)):
            go(Copy(me, hh * group + j, ref.at[1, :, cols(hh)], line.at[j, h, t],
                    s_line.at[step, t], r_line.at[h, t]))
    for pp in range(own):
        p = me * own + pp
        block = p // k
        slot = (block // heads) * k + lax.rem(p, k)
        for c in range(chips):
            go(Copy(me, lax.rem(block, heads) * group + c * 2 + core, saved_ref.at[pp],
                    w1buf.at[slot], s_w.at[pp, c], r_w.at[slot]))

    fwd = []
    for step in (0, 1, 3, 2):
        s = lax.rem(h + step, heads)
        for t in range(2):
            arrived(line.at[j, s, t], r_line.at[s, t])
        for d in range(1, chips):
            cc = lax.rem(chip + d, chips)
            c = pltpu.make_async_remote_copy(
                src_ref=line.at[j, s], dst_ref=line.at[j, s], send_sem=s_fwd.at[d, s],
                recv_sem=r_fwd.at[chip, s], device_id={"ctx": h * group + cc * 2 + core},
                device_id_type=MESH)
            c.start()
            fwd.append(c)
        c = pltpu.make_async_remote_copy(
            src_ref=line.at[j, s], dst_ref=line.at[j, s], send_sem=s_sib.at[chip, s],
            recv_sem=r_sib.at[chip, s], device_id={"ctx": other}, device_id_type=MESH)
        c.start()
        fwd.append(c)

    for m in range(3):
        for r in range(k):
            slot = m * k + r
            owner = ((m * heads + h) * k + r) // own
            arrived(w1buf.at[slot], r_w.at[slot])
            c = pltpu.make_async_remote_copy(
                src_ref=w1buf.at[slot], dst_ref=w1buf.at[slot], send_sem=s_wf.at[slot],
                recv_sem=r_w.at[slot], device_id={"ctx": other}, device_id_type=MESH)

            @pl.when(lax.rem(owner, 2) == core)
            def _():
                c.start()

    for t, ref in ((0, k_ref), (1, v_ref), (2, q_ref), (3, do_ref)):
        for step in (2, 1, 3, 0):
            hh = lax.rem(h + step, heads)
            src = ref.at[:, cols(hh)] if t < 2 else ref.at[0, :, cols(hh)]
            go(Copy(me, hh * group + j, src, rest.at[t, h], s_rest.at[t, step], r_rest.at[t, h]))
    for step in range(heads):
        hh = lax.rem(h + step, heads)
        go(Copy(me, hh * group + j, lr_ref.at[hh], lrs.at[h], s_lr.at[step], r_lr.at[h]))

    def saved(m):
        return w1buf[m * k:(m + 1) * k][:, :grain].reshape(dh, dh)

    def send_back(t, value, out):
        stage[t] = value.astype(BF).reshape(heads, tb, dh)
        for step in (2, 1, 3, 0):
            s = lax.rem(h + step, heads)
            go(Copy(me, s * group + j, stage.at[t, s], out, s_out.at[t, step], r_out.at[t, h]))

    adj[...] = jnp.zeros_like(adj)

    def grad_chunk(jj, mine):
        x = line[jj, :, 0].reshape(heads * tb, dh)
        g = line[jj, :, 1].reshape(heads * tb, dh)
        w1, w3, w2 = saved(0), saved(1), saved(2)
        d_gate, d_up, hidden = query_terms(x, g, w1, w3, w2)
        adj[0] += two(tn, x, d_gate)
        adj[1] += two(tn, x, d_up)
        adj[2] += two(tn, hidden, g)
        if mine:
            send_back(1, two(nt, d_gate, w1) + two(nt, d_up, w3), dq_ref.at[1, :, cols(h)])

    grad_chunk(j, True)
    def chip_step(d, _):
        cc = lax.rem(chip + d, chips)
        jj = cc * 2 + core
        for s in range(heads):
            arrived(line.at[jj, s], r_fwd.at[cc, s])
            pltpu.make_async_remote_copy(
                src_ref=line.at[jj, s], dst_ref=line.at[jj, s], send_sem=s_sib.at[cc, s],
                recv_sem=r_sib.at[cc, s], device_id={"ctx": other}, device_id_type=MESH).start()
        grad_chunk(jj, False)
        return 0

    def sib_step(d, _):
        cc = lax.rem(chip + d, chips)
        jj = cc * 2 + (1 - core)
        for s in range(heads):
            arrived(line.at[jj, s], r_sib.at[cc, s])
        grad_chunk(jj, False)
        return 0

    lax.fori_loop(1, chips, chip_step, 0)
    lax.fori_loop(0, chips, sib_step, 0)

    for c in init_copies:
        c.wait()
    for t in range(4):
        for s in range(heads):
            arrived(rest.at[t, s], r_rest.at[t, s])
    for s in range(heads):
        arrived(lrs.at[s], r_lr.at[s])
    tokens = heads * tb
    w1, w3, w2 = w0buf[0], w0buf[1], w0buf[2]
    first = (j == 0).astype(F32)

    def put(m, value):
        value = value + adj[m] * first
        tot[m * k:(m + 1) * k] = value.reshape(k, grain, dh)

    x, g = rest[2].reshape(tokens, dh), rest[3].reshape(tokens, dh)
    d_gate, d_up, hidden = query_terms(x, g, w1, w3, w2)
    put(0, two(tn, x, d_gate))
    put(1, two(tn, x, d_up))
    put(2, two(tn, hidden, g))
    send_back(0, two(nt, d_gate, w1) + two(nt, d_up, w3), dq_ref.at[0, :, cols(h)])

    keys, vals = rest[0].reshape(tokens, dh), rest[1].reshape(tokens, dh)
    base = base_ref[h]
    eta = jnp.concatenate(
        [jnp.broadcast_to(lrs[s][0:1], (tb, tb)).T[:, 0:1] for s in range(heads)], axis=0) * base
    a1, a3, a2 = split(adj[0]), split(adj[1]), split(adj[2])
    gate, up = nn(keys, w1), nn(keys, w3)
    d_hidden = eta * nt(vals, w2)
    proj1, proj3 = two(nn, keys, a1), two(nn, keys, a3)
    back = eta * two(nt, vals, a2)
    logistic, activated, slope = gate_terms(gate)
    curve = logistic * (1.0 - logistic) * (2.0 + gate * (1.0 - 2.0 * logistic))
    us = up * slope
    mixed = proj1 * us + proj3 * activated
    bar_gate = split(d_hidden * (proj1 * up * curve + proj3 * slope) + back * us)
    bar_up = split(d_hidden * proj1 * slope + back * activated)

    def more(m, value):
        tot[m * k:(m + 1) * k] += value.reshape(k, grain, dh)

    more(0, two(tn, keys, bar_gate))
    more(1, two(tn, keys, bar_up))
    more(2, two(tn, split(eta * mixed), vals))

    half = 3 * k // 2
    halves = []
    for i in range(half):
        c = pltpu.make_async_remote_copy(
            src_ref=tot.at[2 * i + 1 - core], dst_ref=sib.at[i], send_sem=s_half.at[i],
            recv_sem=r_half.at[i], device_id={"ctx": other}, device_id_type=MESH)
        c.start()
        halves.append(c)

    d_scaled = two(nn, split(mixed), w2) + two(nn, split(activated * up), a2)
    send_back(3, eta * d_scaled, dv_ref.at[:, cols(h)])
    rate = jnp.sum(vals.astype(F32) * d_scaled, axis=1, keepdims=True)
    acc = jnp.zeros((8, tb), F32)
    for s in range(heads):
        row = jnp.broadcast_to(rate[s * tb:(s + 1) * tb], (tb, tb)).T[0:8]
        rows[s] = row * base
        acc = acc + row * lrs[s]
    tile[...] = acc
    for step in range(heads):
        s = lax.rem(h + step, heads)
        go(Copy(me, s * group + j, rows.at[s], rate_ref.at[h], s_rate.at[step], r_rate.at[h]))
    for step in range(n):
        go(Copy(me, lax.rem(me + step, n), tile, part_ref.at[me], s_tile.at[step], r_tile.at[me]))

    key_grad = two(nt, bar_gate, w1) + two(nt, bar_up, w3)
    key_grad = key_grad + two(nt, split(d_hidden * us), a1)
    key_grad = key_grad + two(nt, split(d_hidden * activated), a3)
    send_back(2, key_grad, dk_ref.at[:, cols(h)])

    for i in range(half):
        halves[i].wait_recv()
        slot = 2 * i + core
        sib[i] = sib[i] + tot[slot]
        p = ((slot // k) * heads + h) * k + lax.rem(slot, k)
        go(Copy(me, p // own, sib.at[i], fbuf.at[lax.rem(p, own), chip], s_fin.at[i],
                r_fin.at[lax.rem(p, own), chip]))

    for pp in range(own):
        for c in range(chips):
            arrived(fbuf.at[pp, c], r_fin.at[pp, c])
        total = fbuf[pp, 0]
        for c in range(1, chips):
            total = total + fbuf[pp, c]
        fast_ref[pp] = total

    for s in range(heads):
        arrived(dq_ref.at[0, :, cols(s)], r_out.at[0, s])
        arrived(dq_ref.at[1, :, cols(s)], r_out.at[1, s])
        arrived(dk_ref.at[:, cols(s)], r_out.at[2, s])
        arrived(dv_ref.at[:, cols(s)], r_out.at[3, s])
        arrived(rate_ref.at[s], r_rate.at[s])
    for i in range(n):
        arrived(part_ref.at[i], r_tile.at[i])
    for c in sends:
        c.wait_send()
    for c in fwd + halves:
        c.wait_send()
    for d in range(1, chips):
        cc = lax.rem(chip + d, chips)
        for s in range(heads):
            pltpu.make_async_remote_copy(
                src_ref=line.at[cc * 2 + core, s], dst_ref=line.at[cc * 2 + core, s],
                send_sem=s_sib.at[cc, s], recv_sem=r_sib.at[cc, s],
                device_id={"ctx": other}, device_id_type=MESH).wait_send()
    for m in range(3):
        for r in range(k):
            slot = m * k + r
            owner = ((m * heads + h) * k + r) // own

            @pl.when(lax.rem(owner, 2) == core)
            def _():
                pltpu.make_async_remote_copy(
                    src_ref=w1buf.at[slot], dst_ref=w1buf.at[slot], send_sem=s_wf.at[slot],
                    recv_sem=r_w.at[slot], device_id={"ctx": other},
                    device_id_type=MESH).wait_send()


def gcd(a, b):
    while b:
        a, b = b, a % b
    return a


def local(n, queries, keys, values, lr_tok, lr_base, fast_init, fast_saved, dout):
    heads, dh = lr_base.shape[0], fast_init.shape[1]
    share, tb = fast_saved.shape[0], keys.shape[0]
    grain = gcd(share, dh)
    pad = -grain % 16
    k, own = dh // grain, share // grain
    group = n // heads
    chips = group // 2
    slots = 3 * k
    saved = jnp.pad(fast_saved.reshape(own, grain, dh), ((0, 0), (0, pad), (0, 0)))
    lr_rows = jnp.broadcast_to(lr_tok.T[:, None, :], (heads, 8, tb))
    dma = pltpu.SemaphoreType.DMA
    vmem = pl.BlockSpec(memory_space=pltpu.VMEM)
    width = heads * dh
    outs = pl.pallas_call(
        functools.partial(body, (n, heads, group, chips, tb, dh, grain, k, own)),
        out_shape=(
            jax.ShapeDtypeStruct((2, tb, width), BF),
            jax.ShapeDtypeStruct((tb, width), BF),
            jax.ShapeDtypeStruct((tb, width), BF),
            jax.ShapeDtypeStruct((heads, 8, tb), F32),
            jax.ShapeDtypeStruct((n, 8, tb), F32),
            jax.ShapeDtypeStruct((own, grain, dh), F32),
        ),
        in_specs=[vmem] * 5 + [pl.BlockSpec(memory_space=pltpu.SMEM),
                               pl.BlockSpec(memory_space=pl.ANY), vmem],
        out_specs=tuple([vmem] * 6),
        scratch_shapes=[
            pltpu.VMEM((group, heads, 2, tb, dh), BF),
            pltpu.VMEM((4, heads, tb, dh), BF),
            pltpu.VMEM((heads, 8, tb), F32),
            pltpu.VMEM((slots, grain + pad, dh), BF),
            pltpu.VMEM((3, dh, dh), BF),
            pltpu.VMEM((3, dh, dh), F32),
            pltpu.VMEM((slots, grain, dh), F32),
            pltpu.VMEM((slots // 2, grain, dh), F32),
            pltpu.VMEM((own, chips, grain, dh), F32),
            pltpu.VMEM((4, heads, tb, dh), BF),
            pltpu.VMEM((heads, 8, tb), F32),
            pltpu.VMEM((8, tb), F32),
            dma((heads, 2)), dma((heads, 2)),
            dma((chips, heads)), dma((chips, heads)),
            dma((chips, heads)), dma((chips, heads)),
            dma((4, heads)), dma((4, heads)),
            dma((heads,)), dma((heads,)),
            dma((own, chips)), dma((slots,)), dma((slots,)),
            dma((3,)),
            dma((4, heads)), dma((4, heads)),
            dma((heads,)), dma((heads,)),
            dma((n,)), dma((n,)),
            dma((slots // 2,)), dma((slots // 2,)),
            dma((slots // 2,)), dma((own, chips)),
        ],
        compiler_params=pltpu.CompilerParams(
            collective_id=0, has_side_effects=True, vmem_limit_bytes=52 * 2**20),
    )(queries, dout, keys, values, lr_rows, lr_base, fast_init, saved)
    d_queries, d_keys, d_values, rate, part, fast = outs
    d_lr_tok = rate[:, 0, :].T
    base_grad = jnp.sum(part[:, 0, :].reshape(heads, -1), axis=1)
    return (d_queries, d_keys, d_values, d_lr_tok, base_grad, fast.reshape(share, dh))


def solution(mesh):
    both = ("grp", "ctx")
    rows = P(both, None)
    spans = P(None, both, None)
    in_specs = (spans, rows, rows, rows, P(), P(), rows, spans)
    out_specs = (spans, rows, rows, rows, P("grp"), rows)
    return jax.shard_map(
        functools.partial(local, mesh.shape["ctx"]), mesh=mesh, in_specs=in_specs,
        out_specs=out_specs, check_vma=False)
```

time: 346 us -> 137 us (0.40)
  the two profiles are of different devices: /device:TPU:0 before, /device:TPU:25 now
where the time goes in v1:
time: 137 us; the launch traced here: 136 us
  Pallas kernels  124 us (91%)
  local copies, waits for them, and re-layouts  10.3 us (8%)
    pallas_call x1, Pallas kernels, local(): pl.pallas_call(functools.partial(body, (n, heads, group, chips, tb, dh, g...  124 us
    unnamed x12, local copies, waits for them, and re-layouts  8.94 us

profile of v1, /device:TPU:25, one launch (start us, length us, event | category | flops | bytes accessed | tf_op | source)
XLA Modules:
  0.0 136.1 jit_solution(8494712082274103341)
XLA Ops:
  0.6 0.7 broadcast_in_dim.2.lr_ref
  1.3 0.0 copy-start
  1.3 1.0 copy-done
  2.3 0.0 copy-start.1
  2.3 1.0 copy-done.1
  3.3 0.0 copy-start.2
  3.3 0.9 copy-done.2
  4.2 0.0 copy-start.3
  4.2 0.7 copy-done.3
  4.9 124.4 %shard_map.127 = (bf16[2,128,1536]{2,1,0:T(8,128)(2,1)}, bf16[128,1536]{1,0:T(8,128)(2,1)S(1)}, bf16[128,1536]{1,0:T(8,128)(2,1)S(1)}, f32[4,8,128]{2,1,0:T(8,12...) custom-call(bf16[2,128,1536]{2,1,0:T(8,128)(2,1)} %q_ref.1, bf16[2,128,1536]{2,1,0:T(8,128)(2,1)} %do_ref.1, ...), custom_call_target="tpu_custom_call" | custom-call | tf_op jit(solution)/shard_map/pallas_call | solution.py:357
  129.3 0.2 slice_reduce_fusion
  129.5 0.1 reduce_sum.14
  129.6 0.6 reduce_sum.18
  130.2 0.6 slice.6
  130.8 2.1 %copy.18 = bf16[2,128,1536]{2,1,0:T(8,128)(2,1)} copy(bf16[2,128,1536]{2,1,0:T(8,128)(2,1)} %get-tuple-element.24) | data formatting | bytes 1572864
  132.9 0.7 copy.19
  133.6 0.7 copy.20
  134.3 1.8 %copy.21 = f32[288,384]{1,0:T(8,128)} copy(f32[288,384]{1,0:T(8,128)} %bitcast.7) | data formatting | bytes 884736
Async XLA Ops:
  1.3 1.0 copy-start
  2.3 1.0 copy-start.1
  3.3 0.9 copy-start.2
  4.2 0.7 copy-start.3

commit v2 on v1

--- a/solution.py
+++ b/solution.py
@@ -81,10 +81,10 @@
 
 def body(sz, q_ref, do_ref, k_ref, v_ref, lr_ref, base_ref, init_ref, saved_ref,
          dq_ref, dk_ref, dv_ref, rate_ref, part_ref, fast_ref,
-         line, rest, lrs, w1buf, w0buf, adj, tot, sib, fbuf, stage, rows, tile,
+         line, rest, lrs, w1buf, w0buf, adj, tot, sib, ybuf, stage, rows, back_rows, tile,
          s_line, r_line, s_fwd, r_fwd, s_sib, r_sib, s_rest, r_rest, s_lr, r_lr,
-         s_w, r_w, s_wf, r_init, s_out, r_out, s_rate, r_rate, s_tile, r_tile,
-         s_half, r_half, s_fin, r_fin):
+         s_w, r_w, s_wc, s_wf, r_init, s_out, r_out, s_rate, r_rate, s_tile, r_tile,
+         s_half, r_half, s_y, r_y, s_fin, r_fin):
     n, heads, group, chips, tb, dh, grain, k, pieces = sz
     me = lax.axis_index("ctx")
     h = me // group
@@ -113,21 +113,63 @@
         copy.start()
         sends.append(copy)
 
+    for pp in range(own):
+        p = me * own + pp
+        block = p // k
+        slot = (block // heads) * k + lax.rem(p, k)
+        go(Copy(me, lax.rem(block, heads) * group + j, saved_ref.at[pp],
+                w1buf.at[slot], s_w.at[pp], r_w.at[slot]))
     for step in (2, 1, 3, 0):
         hh = lax.rem(h + step, heads)
         for t, ref in ((0, q_ref), (1, do_ref)):
             go(Copy(me, hh * group + j, ref.at[1, :, cols(hh)], line.at[j, h, t],
                     s_line.at[step, t], r_line.at[h, t]))
-    for pp in range(own):
-        p = me * own + pp
-        block = p // k
-        slot = (block // heads) * k + lax.rem(p, k)
-        for c in range(chips):
-            go(Copy(me, lax.rem(block, heads) * group + c * 2 + core, saved_ref.at[pp],
-                    w1buf.at[slot], s_w.at[pp, c], r_w.at[slot]))
+    for s in range(heads):
+        rows[s] = jnp.broadcast_to(lr_ref[s:s + 1, :], (8, tb))
+
+    def w_copy(slot, dest, sem):
+        return pltpu.make_async_remote_copy(
+            src_ref=w1buf.at[slot], dst_ref=w1buf.at[slot], send_sem=sem, recv_sem=r_w.at[slot],
+            device_id={"ctx": dest}, device_id_type=MESH)
+
+    def w_each(fn):
+        for slot in range(3 * k):
+            owner = (((slot // k) * heads + h) * k + slot % k) // own
+            fn(slot, lax.rem(owner, group))
+
+    def w_line(slot, oj):
+        @pl.when(oj == j)
+        def _():
+            arrived(w1buf.at[slot], r_w.at[slot])
+            for d in range(1, chips):
+                w_copy(slot, h * group + lax.rem(chip + d, chips) * 2 + core, s_wc.at[slot, d]).start()
+            w_copy(slot, other, s_wf.at[slot]).start()
+
+    def w_chip(slot, oj):
+        @pl.when(jnp.logical_and(oj != j, lax.rem(oj, 2) == core))
+        def _():
+            arrived(w1buf.at[slot], r_w.at[slot])
+            w_copy(slot, other, s_wf.at[slot]).start()
+
+    def w_last(slot, oj):
+        @pl.when(lax.rem(oj, 2) != core)
+        def _():
+            arrived(w1buf.at[slot], r_w.at[slot])
+
+    def w_sent(slot, oj):
+        @pl.when(oj == j)
+        def _():
+            for d in range(1, chips):
+                w_copy(slot, h * group + lax.rem(chip + d, chips) * 2 + core, s_wc.at[slot, d]).wait_send()
+
+        @pl.when(lax.rem(oj, 2) == core)
+        def _():
+            w_copy(slot, other, s_wf.at[slot]).wait_send()
 
     fwd = []
     for step in (0, 1, 3, 2):
+        if step == 1:
+            w_each(w_line)
         s = lax.rem(h + step, heads)
         for t in range(2):
             arrived(line.at[j, s, t], r_line.at[s, t])
@@ -145,33 +187,26 @@
         c.start()
         fwd.append(c)
 
-    for m in range(3):
-        for r in range(k):
-            slot = m * k + r
-            owner = ((m * heads + h) * k + r) // own
-            arrived(w1buf.at[slot], r_w.at[slot])
-            c = pltpu.make_async_remote_copy(
-                src_ref=w1buf.at[slot], dst_ref=w1buf.at[slot], send_sem=s_wf.at[slot],
-                recv_sem=r_w.at[slot], device_id={"ctx": other}, device_id_type=MESH)
-
-            @pl.when(lax.rem(owner, 2) == core)
-            def _():
-                c.start()
-
-    for t, ref in ((0, k_ref), (1, v_ref), (2, q_ref), (3, do_ref)):
+    w_each(w_chip)
+
+    for step in range(heads):
+        hh = lax.rem(h + step, heads)
+        go(Copy(me, hh * group + j, rows.at[hh], lrs.at[h], s_lr.at[step], r_lr.at[h]))
+    for t, ref in ((2, q_ref), (3, do_ref), (0, k_ref), (1, v_ref)):
         for step in (2, 1, 3, 0):
             hh = lax.rem(h + step, heads)
             src = ref.at[:, cols(hh)] if t < 2 else ref.at[0, :, cols(hh)]
             go(Copy(me, hh * group + j, src, rest.at[t, h], s_rest.at[t, step], r_rest.at[t, h]))
-    for step in range(heads):
-        hh = lax.rem(h + step, heads)
-        go(Copy(me, hh * group + j, lr_ref.at[hh], lrs.at[h], s_lr.at[step], r_lr.at[h]))
+
+    w_each(w_last)
 
     def saved(m):
         return w1buf[m * k:(m + 1) * k][:, :grain].reshape(dh, dh)
 
-    def send_back(t, value, out):
+    def keep(t, value):
         stage[t] = value.astype(BF).reshape(heads, tb, dh)
+
+    def send_back(t, out):
         for step in (2, 1, 3, 0):
             s = lax.rem(h + step, heads)
             go(Copy(me, s * group + j, stage.at[t, s], out, s_out.at[t, step], r_out.at[t, h]))
@@ -187,7 +222,7 @@
         adj[1] += two(tn, x, d_up)
         adj[2] += two(tn, hidden, g)
         if mine:
-            send_back(1, two(nt, d_gate, w1) + two(nt, d_up, w3), dq_ref.at[1, :, cols(h)])
+            keep(1, two(nt, d_gate, w1) + two(nt, d_up, w3))
 
     grad_chunk(j, True)
     def chip_step(d, _):
@@ -214,11 +249,12 @@
 
     for c in init_copies:
         c.wait()
-    for t in range(4):
+    def rest_in(t):
         for s in range(heads):
             arrived(rest.at[t, s], r_rest.at[t, s])
-    for s in range(heads):
-        arrived(lrs.at[s], r_lr.at[s])
+
+    rest_in(2)
+    rest_in(3)
     tokens = heads * tb
     w1, w3, w2 = w0buf[0], w0buf[1], w0buf[2]
     first = (j == 0).astype(F32)
@@ -232,7 +268,13 @@
     put(0, two(tn, x, d_gate))
     put(1, two(tn, x, d_up))
     put(2, two(tn, hidden, g))
-    send_back(0, two(nt, d_gate, w1) + two(nt, d_up, w3), dq_ref.at[0, :, cols(h)])
+    keep(0, two(nt, d_gate, w1) + two(nt, d_up, w3))
+    rest_in(0)
+    rest_in(1)
+    send_back(1, dq_ref.at[1, :, cols(h)])
+    send_back(0, dq_ref.at[0, :, cols(h)])
+    for s in range(heads):
+        arrived(lrs.at[s], r_lr.at[s])
 
     keys, vals = rest[0].reshape(tokens, dh), rest[1].reshape(tokens, dh)
     base = base_ref[h]
@@ -267,41 +309,56 @@
         halves.append(c)
 
     d_scaled = two(nn, split(mixed), w2) + two(nn, split(activated * up), a2)
-    send_back(3, eta * d_scaled, dv_ref.at[:, cols(h)])
+    keep(3, eta * d_scaled)
+    send_back(3, dv_ref.at[:, cols(h)])
     rate = jnp.sum(vals.astype(F32) * d_scaled, axis=1, keepdims=True)
     acc = jnp.zeros((8, tb), F32)
     for s in range(heads):
         row = jnp.broadcast_to(rate[s * tb:(s + 1) * tb], (tb, tb)).T[0:8]
-        rows[s] = row * base
+        back_rows[s] = row * base
         acc = acc + row * lrs[s]
     tile[...] = acc
     for step in range(heads):
         s = lax.rem(h + step, heads)
-        go(Copy(me, s * group + j, rows.at[s], rate_ref.at[h], s_rate.at[step], r_rate.at[h]))
+        go(Copy(me, s * group + j, back_rows.at[s], rate_ref.at[h], s_rate.at[step], r_rate.at[h]))
     for step in range(n):
         go(Copy(me, lax.rem(me + step, n), tile, part_ref.at[me], s_tile.at[step], r_tile.at[me]))
+
+    for i in range(half):
+        halves[i].wait_recv()
+        sib[i] = sib[i] + tot[2 * i + core]
+    per = half // chips
+    for d in range(1, chips):
+        cc = lax.rem(chip + d, chips)
+        for i in range(per):
+            c = pltpu.make_async_remote_copy(
+                src_ref=sib.at[cc * per + i], dst_ref=ybuf.at[i, chips - d], send_sem=s_y.at[i, d],
+                recv_sem=r_y.at[i, chips - d], device_id={"ctx": h * group + cc * 2 + core},
+                device_id_type=MESH)
+            c.start()
+            fwd.append(c)
 
     key_grad = two(nt, bar_gate, w1) + two(nt, bar_up, w3)
     key_grad = key_grad + two(nt, split(d_hidden * us), a1)
     key_grad = key_grad + two(nt, split(d_hidden * activated), a3)
-    send_back(2, key_grad, dk_ref.at[:, cols(h)])
-
-    for i in range(half):
-        halves[i].wait_recv()
-        slot = 2 * i + core
-        sib[i] = sib[i] + tot[slot]
+    keep(2, key_grad)
+    send_back(2, dk_ref.at[:, cols(h)])
+
+    for i in range(per):
+        for d in range(1, chips):
+            arrived(ybuf.at[i, d], r_y.at[i, d])
+        x = chip * per + i
+        total = sib[x]
+        for d in range(1, chips):
+            total = total + ybuf[i, d]
+        ybuf[i, 0] = total
+        slot = 2 * x + core
         p = ((slot // k) * heads + h) * k + lax.rem(slot, k)
-        go(Copy(me, p // own, sib.at[i], fbuf.at[lax.rem(p, own), chip], s_fin.at[i],
-                r_fin.at[lax.rem(p, own), chip]))
+        go(Copy(me, p // own, ybuf.at[i, 0], fast_ref.at[lax.rem(p, own)], s_fin.at[i],
+                r_fin.at[lax.rem(p, own)]))
 
     for pp in range(own):
-        for c in range(chips):
-            arrived(fbuf.at[pp, c], r_fin.at[pp, c])
-        total = fbuf[pp, 0]
-        for c in range(1, chips):
-            total = total + fbuf[pp, c]
-        fast_ref[pp] = total
-
+        arrived(fast_ref.at[pp], r_fin.at[pp])
     for s in range(heads):
         arrived(dq_ref.at[0, :, cols(s)], r_out.at[0, s])
         arrived(dq_ref.at[1, :, cols(s)], r_out.at[1, s])
@@ -321,17 +378,23 @@
                 src_ref=line.at[cc * 2 + core, s], dst_ref=line.at[cc * 2 + core, s],
                 send_sem=s_sib.at[cc, s], recv_sem=r_sib.at[cc, s],
                 device_id={"ctx": other}, device_id_type=MESH).wait_send()
-    for m in range(3):
-        for r in range(k):
-            slot = m * k + r
-            owner = ((m * heads + h) * k + r) // own
-
-            @pl.when(lax.rem(owner, 2) == core)
-            def _():
-                pltpu.make_async_remote_copy(
-                    src_ref=w1buf.at[slot], dst_ref=w1buf.at[slot], send_sem=s_wf.at[slot],
-                    recv_sem=r_w.at[slot], device_id={"ctx": other},
-                    device_id_type=MESH).wait_send()
+    w_each(w_sent)
+
+
+def write_out(group, dq, dk, dv, rate, part, fast, o_dq, o_dk, o_dv, o_rate, o_base, o_fast, sem):
+    own, grain, _ = fast.shape
+    pairs = [(dq.at[0], o_dq.at[0]), (dq.at[1], o_dq.at[1]), (dk, o_dk), (dv, o_dv)]
+    pairs += [(fast.at[i], o_fast.at[pl.ds(i * grain, grain)]) for i in range(own)]
+    copies = [pltpu.make_async_copy(a, b, sem.at[i]) for i, (a, b) in enumerate(pairs)]
+    for c in copies:
+        c.start()
+    heads = rate.shape[0]
+    for s in range(heads):
+        o_rate[s:s + 1, :] = rate[s, 0:1, :]
+    for s in range(heads):
+        o_base[s] = jnp.sum(jnp.sum(part[s * group:(s + 1) * group], axis=0)[0:1])
+    for c in copies:
+        c.wait()
 
 
 def gcd(a, b):
@@ -350,9 +413,9 @@
     chips = group // 2
     slots = 3 * k
     saved = jnp.pad(fast_saved.reshape(own, grain, dh), ((0, 0), (0, pad), (0, 0)))
-    lr_rows = jnp.broadcast_to(lr_tok.T[:, None, :], (heads, 8, tb))
     dma = pltpu.SemaphoreType.DMA
     vmem = pl.BlockSpec(memory_space=pltpu.VMEM)
+    anyw = pl.BlockSpec(memory_space=pl.ANY)
     width = heads * dh
     outs = pl.pallas_call(
         functools.partial(body, (n, heads, group, chips, tb, dh, grain, k, own)),
@@ -364,9 +427,8 @@
             jax.ShapeDtypeStruct((n, 8, tb), F32),
             jax.ShapeDtypeStruct((own, grain, dh), F32),
         ),
-        in_specs=[vmem] * 5 + [pl.BlockSpec(memory_space=pltpu.SMEM),
-                               pl.BlockSpec(memory_space=pl.ANY), vmem],
-        out_specs=tuple([vmem] * 6),
+        in_specs=[anyw] * 4 + [vmem, pl.BlockSpec(memory_space=pltpu.SMEM), anyw, anyw],
+        out_specs=(anyw, anyw, anyw, vmem, vmem, anyw),
         scratch_shapes=[
             pltpu.VMEM((group, heads, 2, tb, dh), BF),
             pltpu.VMEM((4, heads, tb, dh), BF),
@@ -376,8 +438,9 @@
             pltpu.VMEM((3, dh, dh), F32),
             pltpu.VMEM((slots, grain, dh), F32),
             pltpu.VMEM((slots // 2, grain, dh), F32),
-            pltpu.VMEM((own, chips, grain, dh), F32),
+            pltpu.VMEM((slots // 2 // chips, chips, grain, dh), F32),
             pltpu.VMEM((4, heads, tb, dh), BF),
+            pltpu.VMEM((heads, 8, tb), F32),
             pltpu.VMEM((heads, 8, tb), F32),
             pltpu.VMEM((8, tb), F32),
             dma((heads, 2)), dma((heads, 2)),
@@ -385,21 +448,34 @@
             dma((chips, heads)), dma((chips, heads)),
             dma((4, heads)), dma((4, heads)),
             dma((heads,)), dma((heads,)),
-            dma((own, chips)), dma((slots,)), dma((slots,)),
+            dma((own,)), dma((slots,)), dma((slots, chips)), dma((slots,)),
             dma((3,)),
             dma((4, heads)), dma((4, heads)),
             dma((heads,)), dma((heads,)),
             dma((n,)), dma((n,)),
             dma((slots // 2,)), dma((slots // 2,)),
-            dma((slots // 2,)), dma((own, chips)),
+            dma((slots // 2 // chips, chips)), dma((slots // 2 // chips, chips)),
+            dma((slots // 2 // chips,)), dma((own,)),
         ],
         compiler_params=pltpu.CompilerParams(
-            collective_id=0, has_side_effects=True, vmem_limit_bytes=52 * 2**20),
-    )(queries, dout, keys, values, lr_rows, lr_base, fast_init, saved)
-    d_queries, d_keys, d_values, rate, part, fast = outs
-    d_lr_tok = rate[:, 0, :].T
-    base_grad = jnp.sum(part[:, 0, :].reshape(heads, -1), axis=1)
-    return (d_queries, d_keys, d_values, d_lr_tok, base_grad, fast.reshape(share, dh))
+            collective_id=0, has_side_effects=True, vmem_limit_bytes=60 * 2**20),
+    )(queries, dout, keys, values, lr_tok.T, lr_base, fast_init, saved)
+    d_queries, d_keys, d_values, rate, base, fast = pl.pallas_call(
+        functools.partial(write_out, group),
+        out_shape=(
+            jax.ShapeDtypeStruct((2, tb, width), BF),
+            jax.ShapeDtypeStruct((tb, width), BF),
+            jax.ShapeDtypeStruct((tb, width), BF),
+            jax.ShapeDtypeStruct((heads, tb), F32),
+            jax.ShapeDtypeStruct((heads,), F32),
+            jax.ShapeDtypeStruct((share, dh), F32),
+        ),
+        in_specs=[anyw] * 3 + [vmem, vmem, anyw],
+        out_specs=(anyw, anyw, anyw, vmem, pl.BlockSpec(memory_space=pltpu.SMEM), anyw),
+        scratch_shapes=[dma((4 + own,))],
+        compiler_params=pltpu.CompilerParams(vmem_limit_bytes=60 * 2**20),
+    )(*outs)
+    return d_queries, d_keys, d_values, rate.T, base, fast
 
 
 def solution(mesh):

time: 137 us -> 180 us (1.31)
  Pallas kernels: 124 us -> 179 us
  local copies, waits for them, and re-layouts: 10.3 us -> 0 us
    pallas_call x0 -> x1, Pallas kernels: none -> 63.7 us  [local(): pl.pallas_call(functools.partial(write_out, group), out_shape=(jax.ShapeD...]
    pallas_call x1, Pallas kernels: 124 us -> 115 us  [local(): pl.pallas_call(functools.partial(body, (n, heads, group, chips, tb, dh, g...]
    unnamed x12 -> x0, local copies, waits for them, and re-layouts: 8.94 us -> none
where the time goes in v2:
time: 180 us
  Pallas kernels  179 us (99%)
    pallas_call x1, Pallas kernels, local(): pl.pallas_call(functools.partial(body, (n, heads, group, chips, tb, dh, g...  115 us
    pallas_call x1, Pallas kernels, local(): pl.pallas_call(functools.partial(write_out, group), out_shape=(jax.ShapeD...  63.7 us

profile of v2, /device:TPU:25, one launch (start us, length us, event | category | flops | bytes accessed | tf_op | source)
XLA Modules:
  0.0 179.6 jit_solution(10724442862094967939)
XLA Ops:
  0.6 115.1 %shard_map.127 = (bf16[2,128,1536]{2,1,0:T(8,128)(2,1)}, bf16[128,1536]{1,0:T(8,128)(2,1)}, bf16[128,1536]{1,0:T(8,128)(2,1)}, f32[4,8,128]{2,1,0:T(8,128)}, f32...) custom-call(bf16[2,128,1536]{2,1,0:T(8,128)(2,1)} %q_ref.1, bf16[2,128,1536]{2,1,0:T(8,128)(2,1)} %do_ref.1, ...), custom_call_target="tpu_custom_call" | custom-call | tf_op jit(solution)/shard_map/pallas_call | solution.py:420
  115.7 63.7 %shard_map.128 = (bf16[2,128,1536]{2,1,0:T(8,128)(2,1)}, bf16[128,1536]{1,0:T(8,128)(2,1)}, bf16[128,1536]{1,0:T(8,128)(2,1)}, f32[4,128]{1,0:T(4,128)}, f32[4]{0:T(128)}, /*index=5*/f32[288,384]{1,0:T(8,128)}) custom-call(bf16[2,128,1536]{2,1,0:T(8,128)(2,1)} %get-tuple-element.18.dq, bf16[128,1536]{1,0:T(8,128)(2,1)} %get-tuple-element.19.dk, ...), custom_call_target="tpu_custom_call" | custom-call | tf_op jit(solution)/shard_map/pallas_call | solution.py:463

commit v3 on v1

--- a/solution.py
+++ b/solution.py
@@ -353,6 +353,7 @@
     lr_rows = jnp.broadcast_to(lr_tok.T[:, None, :], (heads, 8, tb))
     dma = pltpu.SemaphoreType.DMA
     vmem = pl.BlockSpec(memory_space=pltpu.VMEM)
+    anyw = pl.BlockSpec(memory_space=pl.ANY)
     width = heads * dh
     outs = pl.pallas_call(
         functools.partial(body, (n, heads, group, chips, tb, dh, grain, k, own)),
@@ -364,8 +365,7 @@
             jax.ShapeDtypeStruct((n, 8, tb), F32),
             jax.ShapeDtypeStruct((own, grain, dh), F32),
         ),
-        in_specs=[vmem] * 5 + [pl.BlockSpec(memory_space=pltpu.SMEM),
-                               pl.BlockSpec(memory_space=pl.ANY), vmem],
+        in_specs=[anyw] * 4 + [vmem, pl.BlockSpec(memory_space=pltpu.SMEM), anyw, anyw],
         out_specs=tuple([vmem] * 6),
         scratch_shapes=[
             pltpu.VMEM((group, heads, 2, tb, dh), BF),
@@ -394,7 +394,7 @@
             dma((slots // 2,)), dma((own, chips)),
         ],
         compiler_params=pltpu.CompilerParams(
-            collective_id=0, has_side_effects=True, vmem_limit_bytes=52 * 2**20),
+            collective_id=0, has_side_effects=True, vmem_limit_bytes=60 * 2**20),
     )(queries, dout, keys, values, lr_rows, lr_base, fast_init, saved)
     d_queries, d_keys, d_values, rate, part, fast = outs
     d_lr_tok = rate[:, 0, :].T

time: 137 us -> 137 us (level)
    unnamed x12 -> x4, local copies, waits for them, and re-layouts: 8.94 us -> 7.4 us
where the time goes in v3:
time: 137 us
  Pallas kernels  125 us (91%)
  local copies, waits for them, and re-layouts  10.1 us (7%)
  other arithmetic  1.67 us (1%)
    pallas_call x1, Pallas kernels, local(): pl.pallas_call(functools.partial(body, (n, heads, group, chips, tb, dh, g...  125 us
    unnamed x4, local copies, waits for them, and re-layouts  7.4 us

profile of v3, /device:TPU:25, one launch (start us, length us, event | category | flops | bytes accessed | tf_op | source)
XLA Modules:
  0.0 136.9 jit_solution(15882554108518617708)
XLA Ops:
  0.6 1.3 broadcast_in_dim.2.lr_ref
  1.9 124.5 %shard_map.127 = (bf16[2,128,1536]{2,1,0:T(8,128)(2,1)}, bf16[128,1536]{1,0:T(8,128)(2,1)}, bf16[128,1536]{1,0:T(8,128)(2,1)}, f32[4,8,128]{2,1,0:T(8,128)}, f32...) custom-call(bf16[2,128,1536]{2,1,0:T(8,128)(2,1)} %q_ref.1, bf16[2,128,1536]{2,1,0:T(8,128)(2,1)} %do_ref.1, ...), custom_call_target="tpu_custom_call" | custom-call | tf_op jit(solution)/shard_map/pallas_call | solution.py:358
  126.5 1.0 slice_reduce_fusion
  127.5 0.1 reduce_sum.14
  127.6 0.6 reduce_sum.18
  128.2 1.3 slice.6
  129.5 2.1 %copy.18 = bf16[2,128,1536]{2,1,0:T(8,128)(2,1)} copy(bf16[2,128,1536]{2,1,0:T(8,128)(2,1)} %get-tuple-element.24) | data formatting | bytes 1572864
  131.6 1.8 %copy.19 = bf16[128,1536]{1,0:T(8,128)(2,1)} copy(bf16[128,1536]{1,0:T(8,128)(2,1)} %get-tuple-element.25) | data formatting | bytes 786432
  133.3 1.8 %copy.20 = bf16[128,1536]{1,0:T(8,128)(2,1)} copy(bf16[128,1536]{1,0:T(8,128)(2,1)} %get-tuple-element.26) | data formatting | bytes 786432
  135.1 1.8 %copy.21 = f32[288,384]{1,0:T(8,128)} copy(f32[288,384]{1,0:T(8,128)} %bitcast.6) | data formatting | bytes 884736
